TPU v7x, 512 devices: a whole 4x4x16 slice. The times are simulated.
512 devices in a mesh: mesh: 32 (over z, core), run: 16 (over y, x).
Axes of the slice: x: 4, y: 4, z: 16, core: 2. Of those that a mesh axis runs over, the one named last changes fastest.
Arguments:
- snapshots: bfloat16 [65536, 2048], P('mesh', 'run'), may hold values from -6 to 6
- block_cols: int32 [1024, 16], P('mesh'), may hold values from 0 to 1023, as said below
- mass_blocks: bfloat16 [1024, 64, 1024], P('mesh'), as said below
Outputs:
- gram: float32 [2048, 2048], P('mesh', 'run')
Inputs may be any that keep to these rules, and one draw needn't show every extreme that they name: `block_cols`: block row b names 16 different block columns, the first of them b itself; all lie from 2 blocks before the first block row of shard b // 32 to 2 blocks after its last. In every shard but the first, its first block row names the block 2 before the shard; in every shard but the last, its last block row names the block 2 after it. `mass_blocks`: entry [b, i, k * 64 + j] is row i, column j of the k-th stored block of block row b, in the order of block_cols.
All inputs are finite; a program needn't handle non-finite values.
Results may differ from a plain program's by a relative error of at most 0.00056.
Values may be sent and summed in bfloat16 or wider, within the bound.
A program may use at most 64 MiB of HBM per device.

v0:
```python
import jax
import jax.numpy as jnp
from jax import lax
from jax.sharding import PartitionSpec as P

BLK = 64
HB = 2


def extended(block, sides, width):
    for axis, dim in sides:
        count = lax.axis_size(axis)
        forward = [(i, i + 1) for i in range(count - 1)]
        backward = [(target, source) for source, target in forward]
        low = lax.ppermute(
            lax.slice_in_dim(block, block.shape[dim] - width, None, axis=dim), axis, forward
        )
        high = lax.ppermute(lax.slice_in_dim(block, 0, width, axis=dim), axis, backward)
        block = jnp.concatenate([low, block, high], axis=dim)
    return block


def contract_nodes(left_cols, right_cols):
    return lax.dot_general(
        left_cols, right_cols, (((0,), (0,)), ((), ())), preferred_element_type=jnp.float32
    )


def on_device(snapshots, block_cols, mass_blocks):
    node_count = snapshots.shape[0]
    column_count = snapshots.shape[1]
    blocks_here = node_count // BLK
    stored_count = block_cols.shape[1]
    rim_width = HB * BLK
    padded = extended(snapshots, (("mesh", 0),), rim_width)
    shard_index = lax.axis_index("mesh")
    local_cols = block_cols - (shard_index * blocks_here - HB)
    blocked = padded.reshape(blocks_here + 2 * HB, BLK, column_count)
    picked = blocked[local_cols].reshape(blocks_here, stored_count * BLK, column_count)
    weighted = jnp.einsum("bim,bmc->bic", mass_blocks, picked, preferred_element_type=jnp.float32)
    weighted = weighted.astype(jnp.bfloat16).reshape(node_count, column_count)
    gathered = lax.all_gather(snapshots, "run", axis=1, tiled=True)
    partial_term = contract_nodes(gathered, weighted)
    gram = lax.psum_scatter(partial_term, "mesh", scatter_dimension=0, tiled=True)
    return gram


def solution(mesh):
    placed = (P("mesh", "run"), P("mesh", None), P("mesh", None, None))
    return jax.shard_map(
        on_device, mesh=mesh, in_specs=placed, out_specs=P("mesh", "run"), check_vma=False
    )
```

profile of v0, /device:TPU:2, one launch (start us, length us, event | category | flops | bytes accessed | tf_op | source)
XLA Modules:
  0.0 229.1 jit_solution(6387576160055392372)
XLA Ops:
  6.5 0.0 all-gather.2.cloned.1.call-start
  6.5 0.7 all-gather.2.cloned.1.call-update
  7.3 0.0 reduce-scatter.4.cloned.1.call-start
  7.3 0.8 fusion
  8.1 1.7 collective-permute-start
  9.8 1.3 collective-permute-start.1
  11.1 0.7 compare_select_fusion
  11.8 0.1 copy.7
  11.9 0.1 reshape.14
  12.0 0.0 collective-permute-done
  12.0 2.6 %collective-permute-done.1 = bf16[128,128]{1,0:T(8,128)(2,1)S(1)} collective-permute-done((bf16[128,128]{1,0:T(8,128)(2,1)S(1)}, bf16[128,128]{1,0:T(8,128)(2,1)S(1)}, u32[]{:S(2)}, u32[]{:S(2)}) %collective-permute-start.1) | collective-permute-done | bytes 32800 | tf_op jit(solution)/shard_map/ppermute | solution.py:18
  14.6 1.1 pad_maximum_fusion
  15.7 13.4 %gather_fusion = bf16[512,64,128]{2,1,0:T(8,128)(2,1)} fusion(bf16[36,64,128]{2,1,0:T(8,128)(2,1)S(1)} %bitcast.12, s32[1024]{0:T(1024)S(1)} %pad_clamp_fusion), kind=kCustom, calls=%fused_computation | custom fusion | bytes 16779264 | tf_op jit(solution)/shard_map/gather | solution.py:39
  29.1 6.6 %convolution_convert_fusion = bf16[32,128,64]{1,2,0:T(8,128)(2,1)S(1)} fusion(bf16[32,64,1024]{2,1,0:T(8,128)(2,1)} %param.5, bf16[32,1024,128]{2,1,0:T(8,128)(2,1)} %bitcast.13), kind=kOutput, calls=%fused_computation.2 | convolution fusion | flops 537133056 | bytes 13107200 | tf_op jit(solution)/shard_map/bim,bmc->bic/dot_general | solution.py:40
  35.8 72.4 %all-gather.2.cloned.1.call-done = bf16[2048,2048]{1,0:T(8,128)(2,1)} async-done(((bf16[2048,128]{1,0:T(8,128)(2,1)}), bf16[2048,2048]{1,0:T(8,128)(2,1)}) %all-gather.2.cloned.1.call-update) | async-done | bytes 8388624 | tf_op jit(solution)/shard_map/all_gather | solution.py:42
  108.2 4.7 %convolution_bitcast_fusion = f32[2048,128]{0,1:T(8,128)S(1)} fusion(bf16[2048,128]{1,0:T(8,128)(2,1)S(1)} %bitcast.14, bf16[2048,2048]{1,0:T(8,128)(2,1)} %all-gather.2.cloned.1.call-done), kind=kOutput, calls=%fused_computation.1 | convolution fusion | flops 1073741824 | bytes 9961472 | tf_op jit(solution)/shard_map/dot_general | solution.py:24
  112.9 1.3 copy.9
  114.2 0.0 reduce-scatter.4.cloned.1.call-update
  114.2 108.1 %reduce-scatter.4.cloned.1.call-done = f32[64,128]{1,0:T(8,128)} async-done(((f32[2048,128]{1,0:T(8,128)}), f32[64,128]{1,0:T(8,128)}) %reduce-scatter.4.cloned.1.call-update) | async-done | bytes 32784 | tf_op jit(solution)/shard_map/reduce_scatter | solution.py:44
  (1 shorter events, 0.0 us)
Async XLA Ops:
  6.5 101.7 %all-gather.2.cloned.1.call-start = ((), (), s32[]{:S(2)}) async-start(), calls=%async_computation.1 | async-start | bytes 8912896 | tf_op jit(solution)/shard_map/all_gather | solution.py:42
  7.3 215.0 %reduce-scatter.4.cloned.1.call-start = ((), (), s32[]{:S(2)}) async-start(), calls=%async_computation.2 | async-start | bytes 1081344 | tf_op jit(solution)/shard_map/reduce_scatter | solution.py:44
  8.1 3.9 %collective-permute-start = (bf16[128,128]{1,0:T(8,128)(2,1)S(1)}, bf16[128,128]{1,0:T(8,128)(2,1)S(1)}, u32[]{:S(2)}, u32[]{:S(2)}) collective-permute-start(bf16[128,128]{1,0:T(8,128)(2,1)S(1)} %get-tuple-element.5), channel_id=1, source_target_pairs={{0,16},{16,32},{32,48},{48,64},{64,80},{80,96},{96,112},{112,128},... | collective-permute-start | bytes 98312 | tf_op jit(solution)/shard_map/ppermute | solution.py:15
  9.8 4.8 %collective-permute-start.1 = (bf16[128,128]{1,0:T(8,128)(2,1)S(1)}, bf16[128,128]{1,0:T(8,128)(2,1)S(1)}, u32[]{:S(2)}, u32[]{:S(2)}) collective-permute-start(bf16[128,128]{1,0:T(8,128)(2,1)S(1)} %get-tuple-element.6), channel_id=1, source_target_pairs={{16,0},{32,16},{48,32},{64,48},{80,64},{96,80},{112,96},{128,112},... | collective-permute-start | bytes 98312 | tf_op jit(solution)/shard_map/ppermute | solution.py:18
Sparse Core Ops, SparseCore 0:
  10.3 97.8 all-gather.1
  114.3 107.9 reduce-scatter.3
where the time goes:
time: 229 us
  waiting for transfers between devices  184 us (80%)
  local copies, waits for them, and re-layouts  15.7 us (7%)
  between operations  13.4 us (6%)
  matrix products  11.3 us (5%)
  starting transfers between devices  3.06 us (1%)
    reduce_scatter x1, waiting for transfers between devices, on_device(): lax.psum_scatter(partial_term, 'mesh', scatter_dimension=0, tiled=True)  108 us
    all_gather x1, waiting for transfers between devices, on_device(): gathered = lax.all_gather(snapshots, 'run', axis=1, tiled=True)  72.4 us
    gather x1, local copies, waits for them, and re-layouts, on_device(): blocked[local_cols].reshape(blocks_here, stored_count * BLK, column_count)  13.4 us
    dot_general x1, matrix products, on_device(): jnp.einsum('bim,bmc->bic', mass_blocks, picked, preferred_element_type=jn...  6.61 us
    dot_general x1, matrix products, contract_nodes(): lax.dot_general(left_cols, right_cols, (((0,), (0,)), ((), ())), preferre...  4.66 us
  transfers between devices with their start and end apart: 4, of which 3 were waited for; matrix products, arithmetic and copies ran while one was open for 10% of the time, Pallas kernels for 0%

commit v1 on v0

v1 whole, which is shorter than its diff:
```python
import jax
import jax.numpy as jnp
from jax import lax
from jax.experimental import pallas as pl
from jax.experimental.pallas import tpu as pltpu
from jax.sharding import PartitionSpec as P

BLK = 64
HB = 2
MESH = pl.DeviceIdType.MESH
PARTS = 4


def kernel(
    snap_hbm, cols_hbm, mass_hbm, out_ref,
    cols, ext, sall, wall, mass, acc, comb, zsend, zrecv, red, fin,
    load_sem, halo_ss, halo_rs, s_ss, s_rs, w_ss, w_rs, c_ss, c_rs, z_ss, z_rs, f_ss, f_rs,
):
    m, r = lax.axis_index("mesh"), lax.axis_index("run")
    z, c, y, x = m // 2, m % 2, r // 4, r % 4
    kb, rows_b = cols.shape
    bpc = rows_b // PARTS

    def dev(z_, c_, y_, x_):
        return {"mesh": z_ * 2 + c_, "run": y_ * 4 + x_}

    y_up, y_dn = dev(z, c, (y + 1) % 4, x), dev(z, c, (y + 3) % 4, x)
    x_up, x_dn = dev(z, c, y, (x + 1) % 4), dev(z, c, y, (x + 3) % 4)
    m_up, m_dn = {"mesh": (m + 1) % 32, "run": r}, {"mesh": (m + 31) % 32, "run": r}
    sibling = dev(z, 1 - c, y, x)
    partner = dev((z // 4) * 4 + x, c, y, z % 4)
    moves = (z % 4) != x

    load_ext = pltpu.make_async_copy(snap_hbm, ext.at[pl.ds(HB, rows_b)], load_sem.at[0])
    load_own = pltpu.make_async_copy(snap_hbm, sall.at[y], load_sem.at[1])
    load_ext.start()
    load_own.start()
    load_cols = pltpu.make_async_copy(cols_hbm, cols, load_sem.at[2])
    load_cols.start()
    order = (0, 3, 1, 2)
    loads = {}
    for j in order:
        part = pl.ds(j * bpc, bpc)
        loads[j] = pltpu.make_async_copy(mass_hbm.at[part], mass.at[part], load_sem.at[3 + j])
        loads[j].start()

    barrier = pltpu.get_barrier_semaphore()
    for d in (y_up, y_dn, x_up, x_dn, m_up, m_dn):
        pl.semaphore_signal(barrier, inc=1, device_id=d, device_id_type=MESH)

    def greet(o, _):
        pl.semaphore_signal(barrier, inc=1, device_id=dev((z + o) % 16, c, y, x), device_id_type=MESH)
        return 0

    lax.fori_loop(1, 16, greet, 0)

    @pl.when(moves)
    def _():
        pl.semaphore_signal(barrier, inc=1, device_id=partner, device_id_type=MESH)

    pl.semaphore_wait(barrier, 21 + jnp.where(moves, 1, 0))

    def part_of(way, j):
        return j % PARTS if way == 0 else PARTS - 1 - j % PARTS

    def ring(buf, ss, rs, pos, up, dn, way, j, incoming=False):
        back = 3 if way == 0 else 1
        far = (j // PARTS) + (1 if incoming else 0)
        slot = (pos + back * far) % 4
        rows = pl.ds(part_of(way, j) * bpc, bpc)
        return pltpu.make_async_remote_copy(
            buf.at[slot, rows], buf.at[slot, rows], ss.at[way, j], rs.at[way, j],
            device_id=up if way == 0 else dn, device_id_type=MESH,
        )

    def s_copy(way, j, incoming=False):
        return ring(sall, s_ss, s_rs, y, y_up, y_dn, way, j, incoming)

    def w_copy(way, j, incoming=False):
        return ring(wall, w_ss, w_rs, x, x_up, x_dn, way, j, incoming)

    load_ext.wait()
    halo_up = pltpu.make_async_remote_copy(
        ext.at[pl.ds(rows_b, HB)], ext.at[pl.ds(0, HB)], halo_ss.at[0], halo_rs.at[0],
        device_id=m_up, device_id_type=MESH)
    halo_dn = pltpu.make_async_remote_copy(
        ext.at[pl.ds(HB, HB)], ext.at[pl.ds(rows_b + HB, HB)], halo_ss.at[1], halo_rs.at[1],
        device_id=m_dn, device_id_type=MESH)
    halo_up.start()
    halo_dn.start()
    load_own.wait()
    for j in range(PARTS):
        for way in (0, 1):
            s_copy(way, j).start()

    halo_up.wait_recv()
    halo_dn.wait_recv()
    load_cols.wait()
    base = m * rows_b - HB

    def weigh(b, _):
        picked = jnp.concatenate([ext[jnp.clip(cols[k, b] - base, 0, rows_b + 2 * HB - 1)] for k in range(kb)], axis=0)
        w = jnp.dot(mass[b], picked, preferred_element_type=jnp.float32)
        wall[x, b] = w.astype(jnp.bfloat16)
        return 0

    started = {0: 0, 1: 0}
    have = set()
    for j in order:
        loads[j].wait()
        lax.fori_loop(j * bpc, (j + 1) * bpc, weigh, 0, unroll=4)
        have.add(j)
        for way in (0, 1):
            while started[way] < PARTS and part_of(way, started[way]) in have:
                w_copy(way, started[way]).start()
                started[way] += 1

    for copy in (s_copy, w_copy):
        for j in range(PARTS // 2):
            for way in (0, 1):
                copy(way, j, True).wait_recv()
                copy(way, PARTS + j).start()

    for j in range(PARTS // 2, PARTS + PARTS // 2):
        for way in (0, 1):
            s_copy(way, j, True).wait_recv()

    def gram_part(slot, j, first):
        rows = pl.ds(j * bpc, bpc)
        left = jnp.concatenate([sall[q, rows].reshape(bpc * BLK, 128) for q in range(4)], axis=1)
        right = wall[slot, rows].reshape(bpc * BLK, 128)
        d = lax.dot_general(left, right, (((0,), (0,)), ((), ())), preferred_element_type=jnp.float32)
        d = d.reshape(4, 2, 64, 128)
        if first:
            acc[slot] = d
        else:
            acc[slot] += d

    def combine(slot):
        return pltpu.make_async_remote_copy(
            acc.at[slot, :, 1 - c], comb.at[slot], c_ss.at[slot], c_rs.at[slot],
            device_id=sibling, device_id_type=MESH)

    def z_copy(to, frm):
        return pltpu.make_async_remote_copy(
            zsend.at[to], zrecv.at[frm], z_ss.at[to], z_rs.at[frm],
            device_id=dev(to, c, y, x), device_id_type=MESH)

    def send_off(slot):
        combine(slot).wait_recv()

        def one(q, _):
            zsend[q * 4 + slot] = acc[slot, q, c] + comb[slot, q]

            @pl.when(q * 4 + slot != z)
            def _():
                z_copy(q * 4 + slot, z).start()
            return 0

        lax.fori_loop(0, 4, one, 0)

    slots = [x, (x + 3) % 4, (x + 1) % 4, (x + 2) % 4]
    for i, slot in enumerate(slots):
        if i in (1, 2):
            for j in range(PARTS // 2, PARTS):
                w_copy(i - 1, j, True).wait_recv()
        if i == 3:
            for j in range(PARTS, PARTS + PARTS // 2):
                for way in (0, 1):
                    w_copy(way, j, True).wait_recv()
        for j in range(PARTS):
            gram_part(slot, j, j == 0)
        combine(slot).start()
        if i > 0:
            send_off(slots[i - 1])
    send_off(slots[3])

    red[...] = zsend[z]

    def add(o, _):
        frm = (z + o) % 16
        z_copy(z, frm).wait_recv()
        red[...] += zrecv[frm]
        return 0

    lax.fori_loop(1, 16, add, 0)

    @pl.when(moves)
    def _():
        move = pltpu.make_async_remote_copy(red, fin, f_ss.at[0], f_rs.at[0], device_id=partner, device_id_type=MESH)
        move.start()
        move.wait()
        out_ref[...] = fin[...]

    @pl.when(jnp.logical_not(moves))
    def _():
        out_ref[...] = red[...]

    halo_up.wait_send()
    halo_dn.wait_send()
    for copy in (s_copy, w_copy):
        for j in range(PARTS + PARTS // 2):
            for way in (0, 1):
                copy(way, j).wait_send()
    for slot in range(4):
        combine(slot).wait_send()

    def drain(o, _):
        z_copy((z + o) % 16, z).wait_send()
        return 0

    lax.fori_loop(1, 16, drain, 0)


def on_device(snapshots, block_cols, mass_blocks):
    width = snapshots.shape[1]
    rows_b = block_cols.shape[0]
    snapshots = snapshots.reshape(rows_b, BLK, width)
    dma = pltpu.SemaphoreType.DMA
    steps = PARTS + PARTS // 2
    hbm = pl.BlockSpec(memory_space=pltpu.HBM)
    return pl.pallas_call(
        kernel,
        out_shape=jax.ShapeDtypeStruct((64, width), jnp.float32),
        in_specs=[hbm, hbm, hbm],
        out_specs=pl.BlockSpec(memory_space=pltpu.VMEM),
        scratch_shapes=[
            pltpu.SMEM(block_cols.shape[::-1], jnp.int32),
            pltpu.VMEM((rows_b + 2 * HB, BLK, width), jnp.bfloat16),
            pltpu.VMEM((4, rows_b, BLK, width), jnp.bfloat16),
            pltpu.VMEM((4, rows_b, BLK, width), jnp.bfloat16),
            pltpu.VMEM(mass_blocks.shape, jnp.bfloat16),
            pltpu.VMEM((4, 4, 2, 64, width), jnp.float32),
            pltpu.VMEM((4, 4, 64, width), jnp.float32),
            pltpu.VMEM((16, 64, width), jnp.float32),
            pltpu.VMEM((16, 64, width), jnp.float32),
            pltpu.VMEM((64, width), jnp.float32),
            pltpu.VMEM((64, width), jnp.float32),
            dma((3 + PARTS,)),
            dma((2,)), dma((2,)),
            dma((2, steps)), dma((2, steps)),
            dma((2, steps)), dma((2, steps)),
            dma((4,)), dma((4,)),
            dma((16,)), dma((16,)),
            dma((1,)), dma((1,)),
        ],
        compiler_params=pltpu.CompilerParams(
            collective_id=0, has_side_effects=True, vmem_limit_bytes=60 * 2**20),
        name="gram",
    )(snapshots, block_cols.T, mass_blocks)


def solution(mesh):
    placed = (P("mesh", "run"), P("mesh", None), P("mesh", None, None))
    return jax.shard_map(
        on_device, mesh=mesh, in_specs=placed, out_specs=P("mesh", "run"), check_vma=False
    )
```

time: 229 us -> 70.9 us (0.31)
  the two profiles are of different devices: /device:TPU:2 before, /device:TPU:64 now
where the time goes in v1:
time: 70.9 us; the launch traced here: 70.7 us
  Pallas kernels  69.3 us (98%)
  local copies, waits for them, and re-layouts  1.38 us (2%)
    pallas_call x1, Pallas kernels, on_device(): pl.pallas_call(kernel, out_shape=jax.ShapeDtypeStruct((64, width), jnp.fl...  69.3 us

profile of v1, /device:TPU:64, one launch (start us, length us, event | category | flops | bytes accessed | tf_op | source)
XLA Modules:
  0.0 70.7 jit_solution(2059847363487631988)
XLA Ops:
  0.0 69.3 %gram.1 = f32[64,128]{1,0:T(8,128)} custom-call(bf16[32,64,128]{2,1,0:T(8,128)(2,1)} %bitcast.2, s32[16,32]{1,0:T(8,128)} %bitcast.3, bf16[32,64,1024]{2,1,0:T(8,128)(2,1)} %mass_hbm.1), custom_call_target="tpu_custom_call" | custom-call | tf_op jit(solution)/shard_map/gram/pallas_call | solution.py:222
  69.3 1.4 %copy.5 = f32[64,128]{1,0:T(8,128)} copy(f32[64,128]{1,0:T(8,128)} %gram.1) | data formatting | bytes 65536

commit v2 on v1

--- a/solution.py
+++ b/solution.py
@@ -13,8 +13,8 @@
 
 def kernel(
     snap_hbm, cols_hbm, mass_hbm, out_ref,
-    cols, ext, sall, wall, mass, acc, comb, zsend, zrecv, red, fin,
-    load_sem, halo_ss, halo_rs, s_ss, s_rs, w_ss, w_rs, c_ss, c_rs, z_ss, z_rs, f_ss, f_rs,
+    cols, ext, sall, wall, mass, acc, comb, zsend, merge, zrecv, red, fin,
+    load_sem, halo_ss, halo_rs, s_ss, s_rs, w_ss, w_rs, c_ss, c_rs, m_ss, m_rs, z_ss, z_rs, f_ss, f_rs, relay,
 ):
     m, r = lax.axis_index("mesh"), lax.axis_index("run")
     z, c, y, x = m // 2, m % 2, r // 4, r % 4
@@ -28,8 +28,13 @@
     x_up, x_dn = dev(z, c, y, (x + 1) % 4), dev(z, c, y, (x + 3) % 4)
     m_up, m_dn = {"mesh": (m + 1) % 32, "run": r}, {"mesh": (m + 31) % 32, "run": r}
     sibling = dev(z, 1 - c, y, x)
-    partner = dev((z // 4) * 4 + x, c, y, z % 4)
-    moves = (z % 4) != x
+    z_up, z_dn = dev((z + 1) % 16, c, y, x), dev((z + 15) % 16, c, y, x)
+    home = dev((z // 4) * 4 + x, c, y, (2 * x + 6 - z % 4) % 4)
+    giver = dev((z // 4) * 4 + (2 * (z % 4) + 6 - x) % 4, c, y, z % 4)
+
+    def greet(sem, devices):
+        for d in devices:
+            pl.semaphore_signal(sem, inc=1, device_id=d, device_id_type=MESH)
 
     load_ext = pltpu.make_async_copy(snap_hbm, ext.at[pl.ds(HB, rows_b)], load_sem.at[0])
     load_own = pltpu.make_async_copy(snap_hbm, sall.at[y], load_sem.at[1])
@@ -45,20 +50,15 @@
         loads[j].start()
 
     barrier = pltpu.get_barrier_semaphore()
-    for d in (y_up, y_dn, x_up, x_dn, m_up, m_dn):
-        pl.semaphore_signal(barrier, inc=1, device_id=d, device_id_type=MESH)
-
-    def greet(o, _):
-        pl.semaphore_signal(barrier, inc=1, device_id=dev((z + o) % 16, c, y, x), device_id_type=MESH)
-        return 0
-
-    lax.fori_loop(1, 16, greet, 0)
-
-    @pl.when(moves)
-    def _():
-        pl.semaphore_signal(barrier, inc=1, device_id=partner, device_id_type=MESH)
-
-    pl.semaphore_wait(barrier, 21 + jnp.where(moves, 1, 0))
+    greet(barrier, (y_up, y_dn, x_up, x_dn, m_up, m_dn, z_up, z_dn, home, giver))
+    pl.semaphore_wait(barrier, 10)
+    greet(relay.at[0], (z_up, z_dn))
+
+    def pass_on(i):
+        pl.semaphore_wait(relay.at[i], 2)
+        if i < 2:
+            by = 2 ** (i + 1)
+            greet(relay.at[i + 1], (dev((z + by) % 16, c, y, x), dev((z + 16 - by) % 16, c, y, x)))
 
     def part_of(way, j):
         return j % PARTS if way == 0 else PARTS - 1 - j % PARTS
@@ -95,6 +95,7 @@
 
     halo_up.wait_recv()
     halo_dn.wait_recv()
+    pass_on(0)
     load_cols.wait()
     base = m * rows_b - HB
 
@@ -120,81 +121,124 @@
             for way in (0, 1):
                 copy(way, j, True).wait_recv()
                 copy(way, PARTS + j).start()
-
-    for j in range(PARTS // 2, PARTS + PARTS // 2):
-        for way in (0, 1):
-            s_copy(way, j, True).wait_recv()
-
-    def gram_part(slot, j, first):
+    pass_on(1)
+
+    def left(ps, j):
         rows = pl.ds(j * bpc, bpc)
-        left = jnp.concatenate([sall[q, rows].reshape(bpc * BLK, 128) for q in range(4)], axis=1)
-        right = wall[slot, rows].reshape(bpc * BLK, 128)
-        d = lax.dot_general(left, right, (((0,), (0,)), ((), ())), preferred_element_type=jnp.float32)
-        d = d.reshape(4, 2, 64, 128)
-        if first:
-            acc[slot] = d
-        else:
-            acc[slot] += d
-
-    def combine(slot):
+        return jnp.concatenate([sall[(y + p + 3) % 4, rows].reshape(bpc * BLK, 128) for p in ps], axis=1)
+
+    def right(ps, j):
+        rows = pl.ds(j * bpc, bpc)
+        return jnp.concatenate([wall[(x + p + 3) % 4, rows].reshape(bpc * BLK, 128) for p in ps], axis=1)
+
+    def gram_part(ws, ss, j, first):
+        d = lax.dot_general(left(ss, j), right(ws, j), (((0,), (0,)), ((), ())), preferred_element_type=jnp.float32)
+        for iw, w in enumerate(ws):
+            for i_s, s in enumerate(ss):
+                t = d[128 * i_s:128 * (i_s + 1), 128 * iw:128 * (iw + 1)].reshape(2, 64, 128)
+                if first:
+                    acc[w, s] = t
+                else:
+                    acc[w, s] += t
+
+    near, far = (0, 1, 2), (3,)
+    three = pl.ds(0, 3)
+    groups = (
+        (9, lambda n: n // 3, lambda n: n % 3, (three, three)),
+        (3, lambda n: n, lambda n: 3, (three, 3)),
+        (4, lambda n: 3, lambda n: n, (3, pl.ds(0, 4))),
+    )
+
+    def combine(g):
+        w, s = groups[g][3]
         return pltpu.make_async_remote_copy(
-            acc.at[slot, :, 1 - c], comb.at[slot], c_ss.at[slot], c_rs.at[slot],
-            device_id=sibling, device_id_type=MESH)
+            acc.at[w, s, 1 - c], comb.at[w, s], c_ss.at[g], c_rs.at[g], device_id=sibling, device_id_type=MESH)
+
+    def m_copy(d, o):
+        return pltpu.make_async_remote_copy(
+            zsend.at[d], merge.at[d], m_ss.at[d], m_rs.at[d],
+            device_id=dev((z + jnp.where(o <= 8, 1, 15)) % 16, c, y, x), device_id_type=MESH)
 
     def z_copy(to, frm):
         return pltpu.make_async_remote_copy(
-            zsend.at[to], zrecv.at[frm], z_ss.at[to], z_rs.at[frm],
-            device_id=dev(to, c, y, x), device_id_type=MESH)
-
-    def send_off(slot):
-        combine(slot).wait_recv()
-
-        def one(q, _):
-            zsend[q * 4 + slot] = acc[slot, q, c] + comb[slot, q]
-
-            @pl.when(q * 4 + slot != z)
+            zsend.at[to], zrecv.at[frm], z_ss.at[to], z_rs.at[frm], device_id=dev(to, c, y, x), device_id_type=MESH)
+
+    def chip(w, s):
+        d = ((y + s + 3) % 4) * 4 + (x + 7 - w) % 4
+        return d, (d - z + 16) % 16
+
+    def send_next(g):
+        count, w_of, s_of, _ = groups[g]
+        combine(g).wait_recv()
+
+        def one(n, _):
+            w, s = w_of(n), s_of(n)
+            d, o = chip(w, s)
+            zsend[d] = acc[w, s, c] + comb[w, s]
+
+            @pl.when((o % 2 == 0) & (o != 0))
             def _():
-                z_copy(q * 4 + slot, z).start()
+                m_copy(d, o).start()
             return 0
 
-        lax.fori_loop(0, 4, one, 0)
-
-    slots = [x, (x + 3) % 4, (x + 1) % 4, (x + 2) % 4]
-    for i, slot in enumerate(slots):
-        if i in (1, 2):
-            for j in range(PARTS // 2, PARTS):
-                w_copy(i - 1, j, True).wait_recv()
-        if i == 3:
-            for j in range(PARTS, PARTS + PARTS // 2):
-                for way in (0, 1):
-                    w_copy(way, j, True).wait_recv()
-        for j in range(PARTS):
-            gram_part(slot, j, j == 0)
-        combine(slot).start()
-        if i > 0:
-            send_off(slots[i - 1])
-    send_off(slots[3])
+        lax.fori_loop(0, count, one, 0)
+
+    def send_far(g):
+        count, w_of, s_of, _ = groups[g]
+
+        def one(n, _):
+            d, o = chip(w_of(n), s_of(n))
+
+            @pl.when(o % 2 == 1)
+            def _():
+                @pl.when(o != 9)
+                def _():
+                    m_copy(d, o).wait_recv()
+                    zsend[d] += merge[d]
+                z_copy(d, z).start()
+            return 0
+
+        lax.fori_loop(0, count, one, 0)
+
+    for j in range(PARTS // 2, PARTS):
+        for way in (0, 1):
+            s_copy(way, j, True).wait_recv()
+            w_copy(way, j, True).wait_recv()
+    for j in range(PARTS):
+        gram_part(near, near, j, j == 0)
+    combine(0).start()
+    for j in range(PARTS, PARTS + PARTS // 2):
+        for way in (0, 1):
+            s_copy(way, j, True).wait_recv()
+    for j in range(PARTS):
+        gram_part(near, far, j, j == 0)
+    combine(1).start()
+    send_next(0)
+    send_next(1)
+    pass_on(2)
+    send_far(0)
+    send_far(1)
+    for j in range(PARTS, PARTS + PARTS // 2):
+        for way in (0, 1):
+            w_copy(way, j, True).wait_recv()
+            gram_part(far, near + far, part_of(way, j), j == PARTS and way == 0)
+    combine(2).start()
+    send_next(2)
+    send_far(2)
 
     red[...] = zsend[z]
 
-    def add(o, _):
-        frm = (z + o) % 16
+    def add(n, _):
+        frm = (z + 1 + 2 * n) % 16
         z_copy(z, frm).wait_recv()
         red[...] += zrecv[frm]
         return 0
 
-    lax.fori_loop(1, 16, add, 0)
-
-    @pl.when(moves)
-    def _():
-        move = pltpu.make_async_remote_copy(red, fin, f_ss.at[0], f_rs.at[0], device_id=partner, device_id_type=MESH)
-        move.start()
-        move.wait()
-        out_ref[...] = fin[...]
-
-    @pl.when(jnp.logical_not(moves))
-    def _():
-        out_ref[...] = red[...]
+    lax.fori_loop(0, 8, add, 0)
+    move = pltpu.make_async_remote_copy(red, fin, f_ss.at[0], f_rs.at[0], device_id=home, device_id_type=MESH)
+    move.start()
+    move.wait()
+    out_ref[...] = fin[...]
 
     halo_up.wait_send()
     halo_dn.wait_send()
@@ -202,11 +246,19 @@
         for j in range(PARTS + PARTS // 2):
             for way in (0, 1):
                 copy(way, j).wait_send()
-    for slot in range(4):
-        combine(slot).wait_send()
+    for g in range(3):
+        combine(g).wait_send()
 
     def drain(o, _):
-        z_copy((z + o) % 16, z).wait_send()
+        d = (z + o) % 16
+
+        @pl.when(o % 2 == 0)
+        def _():
+            m_copy(d, o).wait_send()
+
+        @pl.when(o % 2 == 1)
+        def _():
+            z_copy(d, z).wait_send()
         return 0
 
     lax.fori_loop(1, 16, drain, 0)
@@ -234,15 +286,18 @@
             pltpu.VMEM((4, 4, 64, width), jnp.float32),
             pltpu.VMEM((16, 64, width), jnp.float32),
             pltpu.VMEM((16, 64, width), jnp.float32),
+            pltpu.VMEM((16, 64, width), jnp.float32),
             pltpu.VMEM((64, width), jnp.float32),
             pltpu.VMEM((64, width), jnp.float32),
             dma((3 + PARTS,)),
             dma((2,)), dma((2,)),
             dma((2, steps)), dma((2, steps)),
             dma((2, steps)), dma((2, steps)),
-            dma((4,)), dma((4,)),
+            dma((3,)), dma((3,)),
+            dma((16,)), dma((16,)),
             dma((16,)), dma((16,)),
             dma((1,)), dma((1,)),
+            pltpu.SemaphoreType.REGULAR((3,)),
         ],
         compiler_params=pltpu.CompilerParams(
             collective_id=0, has_side_effects=True, vmem_limit_bytes=60 * 2**20),

time: 70.9 us -> 65.2 us (0.920)
  the two profiles are of different devices: /device:TPU:64 before, /device:TPU:88 now
where the time goes in v2:
time: 65.2 us; the launch traced here: 65 us
  Pallas kernels  63.6 us (98%)
  local copies, waits for them, and re-layouts  1.38 us (2%)
    pallas_call x1, Pallas kernels, on_device(): pl.pallas_call(kernel, out_shape=jax.ShapeDtypeStruct((64, width), jnp.fl...  63.6 us
    unnamed x1, local copies, waits for them, and re-layouts  1.38 us

profile of v2, /device:TPU:88, one launch (start us, length us, event | category | flops | bytes accessed | tf_op | source)
XLA Modules:
  0.0 65.0 jit_solution(13356558195399330204)
XLA Ops:
  0.0 63.6 %gram.1 = f32[64,128]{1,0:T(8,128)} custom-call(bf16[32,64,128]{2,1,0:T(8,128)(2,1)} %bitcast.2, s32[16,32]{1,0:T(8,128)} %bitcast.3, bf16[32,64,1024]{2,1,0:T(8,128)(2,1)} %mass_hbm.1), custom_call_target="tpu_custom_call" | custom-call | tf_op jit(solution)/shard_map/gram/pallas_call | solution.py:274
  63.6 1.4 %copy.5 = f32[64,128]{1,0:T(8,128)} copy(f32[64,128]{1,0:T(8,128)} %gram.1) | data formatting | bytes 65536

commit v3 on v2

--- a/solution.py
+++ b/solution.py
@@ -11,9 +11,25 @@
 PARTS = 4
 
 
+SENT = 33
+CODE = 32000.0
+
+
+def code(v):
+    power = jnp.ceil(jnp.log2(jnp.maximum(jnp.max(jnp.abs(v), axis=0, keepdims=True), 1e-30)))
+    q = jnp.round(v * (jnp.exp2(-power) * CODE)).astype(jnp.int32)
+    half = v.shape[0] // 2
+    return (q[:half] << 16) | (q[half:] & 0xFFFF), power.astype(jnp.int32)
+
+
+def decode(pairs, power):
+    q = jnp.concatenate([pairs >> 16, (pairs << 16) >> 16], axis=0)
+    return q.astype(jnp.float32) * (jnp.exp2(power.astype(jnp.float32)) * (1 / CODE))
+
+
 def kernel(
     snap_hbm, cols_hbm, mass_hbm, out_ref,
-    cols, ext, sall, wall, mass, acc, comb, zsend, merge, zrecv, red, fin,
+    cols, ext, sall, wall, mass, acc, comb, share, zsend, merge, zrecv, red, fin,
     load_sem, halo_ss, halo_rs, s_ss, s_rs, w_ss, w_rs, c_ss, c_rs, m_ss, m_rs, z_ss, z_rs, f_ss, f_rs, relay,
 ):
     m, r = lax.axis_index("mesh"), lax.axis_index("run")
@@ -123,13 +139,16 @@
                 copy(way, PARTS + j).start()
     pass_on(1)
 
+    def along_x(p):
+        return p + p // 2 - 2 * (p // 3)
+
     def left(ps, j):
         rows = pl.ds(j * bpc, bpc)
         return jnp.concatenate([sall[(y + p + 3) % 4, rows].reshape(bpc * BLK, 128) for p in ps], axis=1)
 
     def right(ps, j):
         rows = pl.ds(j * bpc, bpc)
-        return jnp.concatenate([wall[(x + p + 3) % 4, rows].reshape(bpc * BLK, 128) for p in ps], axis=1)
+        return jnp.concatenate([wall[(x + along_x(p)) % 4, rows].reshape(bpc * BLK, 128) for p in ps], axis=1)
 
     def gram_part(ws, ss, j, first):
         d = lax.dot_general(left(ss, j), right(ws, j), (((0,), (0,)), ((), ())), preferred_element_type=jnp.float32)
@@ -141,10 +160,11 @@
                 else:
                     acc[w, s] += t
 
-    near, far = (0, 1, 2), (3,)
+    own, beside, near, far = (0,), (1, 2), (0, 1, 2), (3,)
     three = pl.ds(0, 3)
     groups = (
-        (9, lambda n: n // 3, lambda n: n % 3, (three, three)),
+        (3, lambda n: 0, lambda n: n, (0, three)),
+        (6, lambda n: 1 + n // 3, lambda n: n % 3, (pl.ds(1, 2), three)),
         (3, lambda n: n, lambda n: 3, (three, 3)),
         (4, lambda n: 3, lambda n: n, (3, pl.ds(0, 4))),
     )
@@ -154,17 +174,27 @@
         return pltpu.make_async_remote_copy(
             acc.at[w, s, 1 - c], comb.at[w, s], c_ss.at[g], c_rs.at[g], device_id=sibling, device_id_type=MESH)
 
+    sent = pl.ds(0, SENT)
+
+    def put(d, v):
+        pairs, power = code(v)
+        zsend[d, 0:32] = pairs
+        zsend[d, 32:40] = jnp.broadcast_to(power, (8, power.shape[1]))
+
+    def taken(ref, i):
+        return decode(ref[i, 0:32], ref[i, 32:33])
+
     def m_copy(d, o):
         return pltpu.make_async_remote_copy(
-            zsend.at[d], merge.at[d], m_ss.at[d], m_rs.at[d],
+            zsend.at[d, sent], merge.at[d, sent], m_ss.at[d], m_rs.at[d],
             device_id=dev((z + jnp.where(o <= 8, 1, 15)) % 16, c, y, x), device_id_type=MESH)
 
     def z_copy(to, frm):
         return pltpu.make_async_remote_copy(
-            zsend.at[to], zrecv.at[frm], z_ss.at[to], z_rs.at[frm], device_id=dev(to, c, y, x), device_id_type=MESH)
+            zsend.at[to, sent], zrecv.at[frm, sent], z_ss.at[to], z_rs.at[frm], device_id=dev(to, c, y, x), device_id_type=MESH)
 
     def chip(w, s):
-        d = ((y + s + 3) % 4) * 4 + (x + 7 - w) % 4
+        d = ((y + s + 3) % 4) * 4 + (x + 6 - along_x(w)) % 4
         return d, (d - z + 16) % 16
 
     def send_next(g):
@@ -174,10 +204,11 @@
         def one(n, _):
             w, s = w_of(n), s_of(n)
             d, o = chip(w, s)
-            zsend[d] = acc[w, s, c] + comb[w, s]
+            share[d] = acc[w, s, c] + comb[w, s]
 
             @pl.when((o % 2 == 0) & (o != 0))
             def _():
+                put(d, share[d])
                 m_copy(d, o).start()
             return 0
 
@@ -194,44 +225,52 @@
                 @pl.when(o != 9)
                 def _():
                     m_copy(d, o).wait_recv()
-                    zsend[d] += merge[d]
+                    share[d] += taken(merge, d)
+                put(d, share[d])
                 z_copy(d, z).start()
             return 0
 
         lax.fori_loop(0, count, one, 0)
 
-    for j in range(PARTS // 2, PARTS):
-        for way in (0, 1):
-            s_copy(way, j, True).wait_recv()
-            w_copy(way, j, True).wait_recv()
-    for j in range(PARTS):
-        gram_part(near, near, j, j == 0)
+    def arrived(copy, first, last):
+        for j in range(first, last):
+            for way in (0, 1):
+                copy(way, j, True).wait_recv()
+
+    def gram(ws, ss):
+        for j in range(PARTS):
+            gram_part(ws, ss, j, j == 0)
+
+    arrived(s_copy, PARTS // 2, PARTS)
+    gram(own, near)
     combine(0).start()
-    for j in range(PARTS, PARTS + PARTS // 2):
-        for way in (0, 1):
-            s_copy(way, j, True).wait_recv()
-    for j in range(PARTS):
-        gram_part(near, far, j, j == 0)
+    send_next(0)
+    arrived(w_copy, PARTS // 2, PARTS)
+    gram(beside, near)
     combine(1).start()
-    send_next(0)
-    send_next(1)
     pass_on(2)
     send_far(0)
+    send_next(1)
+    arrived(s_copy, PARTS, PARTS + PARTS // 2)
+    gram(near, far)
+    combine(2).start()
+    send_next(2)
     send_far(1)
     for j in range(PARTS, PARTS + PARTS // 2):
         for way in (0, 1):
             w_copy(way, j, True).wait_recv()
             gram_part(far, near + far, part_of(way, j), j == PARTS and way == 0)
-    combine(2).start()
-    send_next(2)
+    combine(3).start()
     send_far(2)
-
-    red[...] = zsend[z]
+    send_next(3)
+    send_far(3)
+
+    red[...] = share[z]
 
     def add(n, _):
         frm = (z + 1 + 2 * n) % 16
         z_copy(z, frm).wait_recv()
-        red[...] += zrecv[frm]
+        red[...] += taken(zrecv, frm)
         return 0
 
     lax.fori_loop(0, 8, add, 0)
@@ -246,7 +285,7 @@
         for j in range(PARTS + PARTS // 2):
             for way in (0, 1):
                 copy(way, j).wait_send()
-    for g in range(3):
+    for g in range(4):
         combine(g).wait_send()
 
     def drain(o, _):
@@ -285,15 +324,16 @@
             pltpu.VMEM((4, 4, 2, 64, width), jnp.float32),
             pltpu.VMEM((4, 4, 64, width), jnp.float32),
             pltpu.VMEM((16, 64, width), jnp.float32),
-            pltpu.VMEM((16, 64, width), jnp.float32),
-            pltpu.VMEM((16, 64, width), jnp.float32),
+            pltpu.VMEM((16, 40, width), jnp.int32),
+            pltpu.VMEM((16, 40, width), jnp.int32),
+            pltpu.VMEM((16, 40, width), jnp.int32),
             pltpu.VMEM((64, width), jnp.float32),
             pltpu.VMEM((64, width), jnp.float32),
             dma((3 + PARTS,)),
             dma((2,)), dma((2,)),
             dma((2, steps)), dma((2, steps)),
             dma((2, steps)), dma((2, steps)),
-            dma((3,)), dma((3,)),
+            dma((4,)), dma((4,)),
             dma((16,)), dma((16,)),
             dma((16,)), dma((16,)),
             dma((1,)), dma((1,)),

time: 65.2 us -> 56.7 us (0.87)
  Pallas kernels: 63.6 us -> 55.2 us
    pallas_call x1, Pallas kernels: 63.6 us -> 55.2 us  [on_device(): pl.pallas_call(kernel, out_shape=jax.ShapeDtypeStruct((64, width), jnp.fl...]
where the time goes in v3:
time: 56.7 us; the launch traced here: 56.5 us
  Pallas kernels  55.2 us (97%)
  local copies, waits for them, and re-layouts  1.38 us (2%)
    pallas_call x1, Pallas kernels, on_device(): pl.pallas_call(kernel, out_shape=jax.ShapeDtypeStruct((64, width), jnp.fl...  55.2 us
    unnamed x1, local copies, waits for them, and re-layouts  1.38 us

profile of v3, /device:TPU:88, one launch (start us, length us, event | category | flops | bytes accessed | tf_op | source)
XLA Modules:
  0.0 56.5 jit_solution(18314775523613153337)
XLA Ops:
  0.0 55.2 %gram.1 = f32[64,128]{1,0:T(8,128)} custom-call(bf16[32,64,128]{2,1,0:T(8,128)(2,1)} %bitcast.2, s32[16,32]{1,0:T(8,128)} %bitcast.3, bf16[32,64,1024]{2,1,0:T(8,128)(2,1)} %mass_hbm.1), custom_call_target="tpu_custom_call" | custom-call | tf_op jit(solution)/shard_map/gram/pallas_call | solution.py:313
  55.2 1.4 %copy.5 = f32[64,128]{1,0:T(8,128)} copy(f32[64,128]{1,0:T(8,128)} %gram.1) | data formatting | bytes 65536

commit v4 on v3

--- a/solution.py
+++ b/solution.py
@@ -16,21 +16,21 @@
 
 
 def code(v):
-    power = jnp.ceil(jnp.log2(jnp.maximum(jnp.max(jnp.abs(v), axis=0, keepdims=True), 1e-30)))
+    power = jnp.ceil(jnp.log2(jnp.maximum(jnp.max(jnp.abs(v), axis=1, keepdims=True), 1e-30)))
     q = jnp.round(v * (jnp.exp2(-power) * CODE)).astype(jnp.int32)
-    half = v.shape[0] // 2
-    return (q[:half] << 16) | (q[half:] & 0xFFFF), power.astype(jnp.int32)
+    half = v.shape[1] // 2
+    return (q[:, :half] << 16) | (q[:, half:] & 0xFFFF), power.astype(jnp.int32)
 
 
 def decode(pairs, power):
-    q = jnp.concatenate([pairs >> 16, (pairs << 16) >> 16], axis=0)
+    q = jnp.concatenate([pairs >> 16, (pairs << 16) >> 16], axis=1)
     return q.astype(jnp.float32) * (jnp.exp2(power.astype(jnp.float32)) * (1 / CODE))
 
 
 def kernel(
     snap_hbm, cols_hbm, mass_hbm, out_ref,
-    cols, ext, sall, wall, mass, acc, comb, share, zsend, merge, zrecv, red, fin,
-    load_sem, halo_ss, halo_rs, s_ss, s_rs, w_ss, w_rs, c_ss, c_rs, m_ss, m_rs, z_ss, z_rs, f_ss, f_rs, relay,
+    cols, ext, sall, wall, mass, acc, comb, share, coded, zrecv, red, fin,
+    load_sem, halo_ss, halo_rs, s_ss, s_rs, w_ss, w_rs, c_ss, c_rs, z_ss, z_rs, f_ss, f_rs, relay,
 ):
     m, r = lax.axis_index("mesh"), lax.axis_index("run")
     z, c, y, x = m // 2, m % 2, r // 4, r % 4
@@ -51,6 +51,9 @@
     def greet(sem, devices):
         for d in devices:
             pl.semaphore_signal(sem, inc=1, device_id=d, device_id_type=MESH)
+
+    barrier = pltpu.get_barrier_semaphore()
+    greet(barrier, (y_up, y_dn, x_up, x_dn, m_up, m_dn, z_up, z_dn))
 
     load_ext = pltpu.make_async_copy(snap_hbm, ext.at[pl.ds(HB, rows_b)], load_sem.at[0])
     load_own = pltpu.make_async_copy(snap_hbm, sall.at[y], load_sem.at[1])
@@ -65,13 +68,11 @@
         loads[j] = pltpu.make_async_copy(mass_hbm.at[part], mass.at[part], load_sem.at[3 + j])
         loads[j].start()
 
-    barrier = pltpu.get_barrier_semaphore()
-    greet(barrier, (y_up, y_dn, x_up, x_dn, m_up, m_dn, z_up, z_dn, home, giver))
-    pl.semaphore_wait(barrier, 10)
-    greet(relay.at[0], (z_up, z_dn))
+    pl.semaphore_wait(barrier, 8)
+    greet(relay.at[0], (z_up, z_dn, x_up, x_dn, sibling))
 
     def pass_on(i):
-        pl.semaphore_wait(relay.at[i], 2)
+        pl.semaphore_wait(relay.at[i], 5 if i == 0 else 2)
         if i < 2:
             by = 2 ** (i + 1)
             greet(relay.at[i + 1], (dev((z + by) % 16, c, y, x), dev((z + 16 - by) % 16, c, y, x)))
@@ -137,7 +138,8 @@
             for way in (0, 1):
                 copy(way, j, True).wait_recv()
                 copy(way, PARTS + j).start()
-    pass_on(1)
+        if copy is s_copy:
+            pass_on(1)
 
     def along_x(p):
         return p + p // 2 - 2 * (p // 3)
@@ -176,61 +178,47 @@
 
     sent = pl.ds(0, SENT)
 
-    def put(d, v):
-        pairs, power = code(v)
-        zsend[d, 0:32] = pairs
-        zsend[d, 32:40] = jnp.broadcast_to(power, (8, power.shape[1]))
-
-    def taken(ref, i):
-        return decode(ref[i, 0:32], ref[i, 32:33])
-
-    def m_copy(d, o):
+    def put(ref, v, *at):
+        pairs, power = code(v.reshape(-1, *v.shape[-2:]))
+        lead = v.shape[:-2]
+        ref[*at, 0:32] = pairs.reshape(*lead, *pairs.shape[1:])
+        ref[*at, 32:40] = jnp.broadcast_to(power, (power.shape[0], 8, power.shape[2])).reshape(*lead, 8, power.shape[2])
+
+    def taken(ref, *at):
+        pairs, power = ref[*at, 0:32], ref[*at, 32:33]
+        lead = pairs.shape[:-2]
+        v = decode(pairs.reshape(-1, *pairs.shape[-2:]), power.reshape(-1, *power.shape[-2:]))
+        return v.reshape(*lead, *v.shape[1:])
+
+    def z_copy(w, s, to, frm):
         return pltpu.make_async_remote_copy(
-            zsend.at[d, sent], merge.at[d, sent], m_ss.at[d], m_rs.at[d],
-            device_id=dev((z + jnp.where(o <= 8, 1, 15)) % 16, c, y, x), device_id_type=MESH)
-
-    def z_copy(to, frm):
-        return pltpu.make_async_remote_copy(
-            zsend.at[to, sent], zrecv.at[frm, sent], z_ss.at[to], z_rs.at[frm], device_id=dev(to, c, y, x), device_id_type=MESH)
+            coded.at[w, s, sent], zrecv.at[frm, sent], z_ss.at[w, s], z_rs.at[frm],
+            device_id=dev(to, c, y, x), device_id_type=MESH)
 
     def chip(w, s):
         d = ((y + s + 3) % 4) * 4 + (x + 6 - along_x(w)) % 4
         return d, (d - z + 16) % 16
 
-    def send_next(g):
-        count, w_of, s_of, _ = groups[g]
+    def each(g, body):
+        def one(n, _):
+            w, s = groups[g][1](n), groups[g][2](n)
+            body(w, s, *chip(w, s))
+            return 0
+
+        lax.fori_loop(0, groups[g][0], one, 0)
+
+    def send(g):
+        at = groups[g][3]
         combine(g).wait_recv()
-
-        def one(n, _):
-            w, s = w_of(n), s_of(n)
-            d, o = chip(w, s)
-            share[d] = acc[w, s, c] + comb[w, s]
-
-            @pl.when((o % 2 == 0) & (o != 0))
+        share[*at] = acc[*at, c] + comb[*at]
+        put(coded, share[*at], *at)
+
+        def one(w, s, d, o):
+            @pl.when(o != 0)
             def _():
-                put(d, share[d])
-                m_copy(d, o).start()
-            return 0
-
-        lax.fori_loop(0, count, one, 0)
-
-    def send_far(g):
-        count, w_of, s_of, _ = groups[g]
-
-        def one(n, _):
-            d, o = chip(w_of(n), s_of(n))
-
-            @pl.when(o % 2 == 1)
-            def _():
-                @pl.when(o != 9)
-                def _():
-                    m_copy(d, o).wait_recv()
-                    share[d] += taken(merge, d)
-                put(d, share[d])
-                z_copy(d, z).start()
-            return 0
-
-        lax.fori_loop(0, count, one, 0)
+                z_copy(w, s, d, z).start()
+
+        each(g, one)
 
     def arrived(copy, first, last):
         for j in range(first, last):
@@ -244,36 +232,33 @@
     arrived(s_copy, PARTS // 2, PARTS)
     gram(own, near)
     combine(0).start()
-    send_next(0)
+    pass_on(2)
+    send(0)
     arrived(w_copy, PARTS // 2, PARTS)
     gram(beside, near)
     combine(1).start()
-    pass_on(2)
-    send_far(0)
-    send_next(1)
     arrived(s_copy, PARTS, PARTS + PARTS // 2)
     gram(near, far)
     combine(2).start()
-    send_next(2)
-    send_far(1)
+    send(1)
+    send(2)
     for j in range(PARTS, PARTS + PARTS // 2):
         for way in (0, 1):
             w_copy(way, j, True).wait_recv()
             gram_part(far, near + far, part_of(way, j), j == PARTS and way == 0)
     combine(3).start()
-    send_far(2)
-    send_next(3)
-    send_far(3)
-
-    red[...] = share[z]
+    send(3)
+
+    red[...] = share[along_x((x + 6 - z % 4) % 4), (z // 4 - y + 5) % 4]
 
     def add(n, _):
-        frm = (z + 1 + 2 * n) % 16
-        z_copy(z, frm).wait_recv()
-        red[...] += taken(zrecv, frm)
+        by = n // 2 + 1
+        frm = (z + by + (n % 2) * (16 - 2 * by)) % 16
+        z_copy(0, 0, z, frm).wait_recv()
+        red[...] += taken(zrecv, pl.ds(frm, 1)).reshape(red.shape)
         return 0
 
-    lax.fori_loop(0, 8, add, 0)
+    lax.fori_loop(0, 15, add, 0)
     move = pltpu.make_async_remote_copy(red, fin, f_ss.at[0], f_rs.at[0], device_id=home, device_id_type=MESH)
     move.start()
     move.wait()
@@ -288,19 +273,13 @@
     for g in range(4):
         combine(g).wait_send()
 
-    def drain(o, _):
-        d = (z + o) % 16
-
-        @pl.when(o % 2 == 0)
+    def drain(w, s, d, o):
+        @pl.when(o != 0)
         def _():
-            m_copy(d, o).wait_send()
-
-        @pl.when(o % 2 == 1)
-        def _():
-            z_copy(d, z).wait_send()
-        return 0
-
-    lax.fori_loop(1, 16, drain, 0)
+            z_copy(w, s, d, z).wait_send()
+
+    for g in range(4):
+        each(g, drain)
 
 
 def on_device(snapshots, block_cols, mass_blocks):
@@ -323,9 +302,8 @@
             pltpu.VMEM(mass_blocks.shape, jnp.bfloat16),
             pltpu.VMEM((4, 4, 2, 64, width), jnp.float32),
             pltpu.VMEM((4, 4, 64, width), jnp.float32),
-            pltpu.VMEM((16, 64, width), jnp.float32),
-            pltpu.VMEM((16, 40, width), jnp.int32),
-            pltpu.VMEM((16, 40, width), jnp.int32),
+            pltpu.VMEM((4, 4, 64, width), jnp.float32),
+            pltpu.VMEM((4, 4, 40, width), jnp.int32),
             pltpu.VMEM((16, 40, width), jnp.int32),
             pltpu.VMEM((64, width), jnp.float32),
             pltpu.VMEM((64, width), jnp.float32),
@@ -334,8 +312,7 @@
             dma((2, steps)), dma((2, steps)),
             dma((2, steps)), dma((2, steps)),
             dma((4,)), dma((4,)),
-            dma((16,)), dma((16,)),
-            dma((16,)), dma((16,)),
+            dma((4, 4)), dma((16,)),
             dma((1,)), dma((1,)),
             pltpu.SemaphoreType.REGULAR((3,)),
         ],

time: 56.7 us -> 54.3 us (0.958)
  the two profiles are of different devices: /device:TPU:88 before, /device:TPU:4 now
where the time goes in v4:
time: 54.3 us; the launch traced here: 54.1 us
  Pallas kernels  52.7 us (97%)
  local copies, waits for them, and re-layouts  1.38 us (3%)
    pallas_call x1, Pallas kernels, on_device(): pl.pallas_call(kernel, out_shape=jax.ShapeDtypeStruct((64, width), jnp.fl...  52.7 us
    unnamed x1, local copies, waits for them, and re-layouts  1.38 us

profile of v4, /device:TPU:4, one launch (start us, length us, event | category | flops | bytes accessed | tf_op | source)
XLA Modules:
  0.0 54.1 jit_solution(639461171558700333)
XLA Ops:
  0.0 52.7 %gram.1 = f32[64,128]{1,0:T(8,128)} custom-call(bf16[32,64,128]{2,1,0:T(8,128)(2,1)} %bitcast.2, s32[16,32]{1,0:T(8,128)} %bitcast.3, bf16[32,64,1024]{2,1,0:T(8,128)(2,1)} %mass_hbm.1), custom_call_target="tpu_custom_call" | custom-call | tf_op jit(solution)/shard_map/gram/pallas_call | solution.py:292
  52.7 1.4 %copy.5 = f32[64,128]{1,0:T(8,128)} copy(f32[64,128]{1,0:T(8,128)} %gram.1) | data formatting | bytes 65536

commit v5 on v4

--- a/solution.py
+++ b/solution.py
@@ -45,8 +45,10 @@
     m_up, m_dn = {"mesh": (m + 1) % 32, "run": r}, {"mesh": (m + 31) % 32, "run": r}
     sibling = dev(z, 1 - c, y, x)
     z_up, z_dn = dev((z + 1) % 16, c, y, x), dev((z + 15) % 16, c, y, x)
-    home = dev((z // 4) * 4 + x, c, y, (2 * x + 6 - z % 4) % 4)
-    giver = dev((z // 4) * 4 + (2 * (z % 4) + 6 - x) % 4, c, y, z % 4)
+    over = (x + 2) % 4
+    turn = (z % 4 + 4 - x) % 4
+    back = jnp.where(turn == 1, 15, jnp.where(turn == 3, 1, 0))
+    partner = dev((z + back) % 16, c, y, (x + jnp.where(turn == 1, 1, 3)) % 4)
 
     def greet(sem, devices):
         for d in devices:
@@ -72,10 +74,12 @@
     greet(relay.at[0], (z_up, z_dn, x_up, x_dn, sibling))
 
     def pass_on(i):
-        pl.semaphore_wait(relay.at[i], 5 if i == 0 else 2)
+        pl.semaphore_wait(relay.at[i], (5, 2, 2, 1)[i])
         if i < 2:
             by = 2 ** (i + 1)
             greet(relay.at[i + 1], (dev((z + by) % 16, c, y, x), dev((z + 16 - by) % 16, c, y, x)))
+        elif i == 2:
+            greet(relay.at[3], (dev(z, c, y, over),))
 
     def part_of(way, j):
         return j % PARTS if way == 0 else PARTS - 1 - j % PARTS
@@ -106,9 +110,24 @@
     halo_up.start()
     halo_dn.start()
     load_own.wait()
-    for j in range(PARTS):
-        for way in (0, 1):
-            s_copy(way, j).start()
+    half, whole, rest = range(PARTS // 2), range(PARTS // 2, PARTS), range(PARTS, PARTS + PARTS // 2)
+
+    def begin(copy, steps):
+        for j in steps:
+            for way in (0, 1):
+                copy(way, j).start()
+
+    def left_here(copy, steps):
+        for j in steps:
+            for way in (0, 1):
+                copy(way, j).wait_send()
+
+    def arrived(copy, steps):
+        for j in steps:
+            for way in (0, 1):
+                copy(way, j, True).wait_recv()
+
+    begin(s_copy, half)
 
     halo_up.wait_recv()
     halo_dn.wait_recv()
@@ -129,17 +148,17 @@
         lax.fori_loop(j * bpc, (j + 1) * bpc, weigh, 0, unroll=4)
         have.add(j)
         for way in (0, 1):
-            while started[way] < PARTS and part_of(way, started[way]) in have:
+            while started[way] < PARTS // 2 and part_of(way, started[way]) in have:
                 w_copy(way, started[way]).start()
                 started[way] += 1
 
-    for copy in (s_copy, w_copy):
-        for j in range(PARTS // 2):
-            for way in (0, 1):
-                copy(way, j, True).wait_recv()
-                copy(way, PARTS + j).start()
-        if copy is s_copy:
-            pass_on(1)
+    begin(s_copy, whole)
+    arrived(s_copy, half)
+    begin(w_copy, whole)
+    pass_on(1)
+    left_here(s_copy, whole)
+    begin(s_copy, rest)
+    arrived(w_copy, half)
 
     def along_x(p):
         return p + p // 2 - 2 * (p // 3)
@@ -162,13 +181,14 @@
                 else:
                     acc[w, s] += t
 
-    own, beside, near, far = (0,), (1, 2), (0, 1, 2), (3,)
+    near, far = (0, 1, 2), (3,)
     three = pl.ds(0, 3)
     groups = (
         (3, lambda n: 0, lambda n: n, (0, three)),
-        (6, lambda n: 1 + n // 3, lambda n: n % 3, (pl.ds(1, 2), three)),
+        (3, lambda n: 1, lambda n: n, (1, three)),
+        (3, lambda n: 2, lambda n: n, (2, three)),
         (3, lambda n: n, lambda n: 3, (three, 3)),
-        (4, lambda n: 3, lambda n: n, (3, pl.ds(0, 4))),
+        (4, lambda n: 3, lambda n: (z // 4 + along_x(n) + 7 - y) % 4, (3, pl.ds(0, 4))),
     )
 
     def combine(g):
@@ -190,13 +210,13 @@
         v = decode(pairs.reshape(-1, *pairs.shape[-2:]), power.reshape(-1, *power.shape[-2:]))
         return v.reshape(*lead, *v.shape[1:])
 
-    def z_copy(w, s, to, frm):
+    def z_copy(w, s, to, frm, column=x):
         return pltpu.make_async_remote_copy(
             coded.at[w, s, sent], zrecv.at[frm, sent], z_ss.at[w, s], z_rs.at[frm],
-            device_id=dev(to, c, y, x), device_id_type=MESH)
+            device_id=dev(to, c, y, column), device_id_type=MESH)
 
     def chip(w, s):
-        d = ((y + s + 3) % 4) * 4 + (x + 6 - along_x(w)) % 4
+        d = (((y + s + 3) % 4) * 4 + x + 16 + w % 3 - w % 3 // 2 * 3) % 16
         return d, (d - z + 16) % 16
 
     def each(g, body):
@@ -214,71 +234,91 @@
         put(coded, share[*at], *at)
 
         def one(w, s, d, o):
-            @pl.when(o != 0)
-            def _():
-                z_copy(w, s, d, z).start()
+            if g == 4:
+                z_copy(w, s, d, z, over).start()
+            else:
+                @pl.when(o != 0)
+                def _():
+                    z_copy(w, s, d, z).start()
 
         each(g, one)
-
-    def arrived(copy, first, last):
-        for j in range(first, last):
-            for way in (0, 1):
-                copy(way, j, True).wait_recv()
 
     def gram(ws, ss):
         for j in range(PARTS):
             gram_part(ws, ss, j, j == 0)
 
-    arrived(s_copy, PARTS // 2, PARTS)
-    gram(own, near)
+    arrived(s_copy, whole)
+    gram((0,), near)
     combine(0).start()
+    left_here(w_copy, whole)
+    begin(w_copy, rest)
     pass_on(2)
     send(0)
-    arrived(w_copy, PARTS // 2, PARTS)
-    gram(beside, near)
-    combine(1).start()
-    arrived(s_copy, PARTS, PARTS + PARTS // 2)
+    for way in (0, 1):
+        for j in range(PARTS // 2, PARTS):
+            w_copy(way, j, True).wait_recv()
+        gram((2 - way,), near)
+        combine(2 - way).start()
+    send(2)
+    send(1)
+    arrived(s_copy, rest)
     gram(near, far)
-    combine(2).start()
-    send(1)
-    send(2)
+    combine(3).start()
+    pass_on(3)
+    send(3)
     for j in range(PARTS, PARTS + PARTS // 2):
         for way in (0, 1):
             w_copy(way, j, True).wait_recv()
             gram_part(far, near + far, part_of(way, j), j == PARTS and way == 0)
-    combine(3).start()
-    send(3)
-
-    red[...] = share[along_x((x + 6 - z % 4) % 4), (z // 4 - y + 5) % 4]
-
-    def add(n, _):
-        by = n // 2 + 1
-        frm = (z + by + (n % 2) * (16 - 2 * by)) % 16
-        z_copy(0, 0, z, frm).wait_recv()
-        red[...] += taken(zrecv, pl.ds(frm, 1)).reshape(red.shape)
+    combine(4).start()
+    send(4)
+
+    @pl.when(turn == 2)
+    def _():
+        z_copy(0, 0, z, z).wait_recv()
+        red[...] = taken(zrecv, pl.ds(z, 1)).reshape(red.shape)
+
+    @pl.when(turn != 2)
+    def _():
+        red[...] = share[turn - turn // 3, ((z + back) % 16 // 4 - y + 5) % 4]
+
+    def add(by, _):
+        up, dn = (z + by) % 16, (z + 16 - by) % 16
+        z_copy(0, 0, z, up).wait_recv()
+        z_copy(0, 0, z, dn).wait_recv()
+        red[...] += (taken(zrecv, pl.ds(up, 1)) + taken(zrecv, pl.ds(dn, 1))).reshape(red.shape)
         return 0
 
-    lax.fori_loop(0, 15, add, 0)
-    move = pltpu.make_async_remote_copy(red, fin, f_ss.at[0], f_rs.at[0], device_id=home, device_id_type=MESH)
-    move.start()
-    move.wait()
-    out_ref[...] = fin[...]
+    lax.fori_loop(1, 8, add, 0)
+    z_copy(0, 0, z, (z + 8) % 16).wait_recv()
+    red[...] += taken(zrecv, pl.ds((z + 8) % 16, 1)).reshape(red.shape)
+
+    @pl.when(turn % 2 == 1)
+    def _():
+        move = pltpu.make_async_remote_copy(
+            red, fin, f_ss.at[0], f_rs.at[0], device_id=partner, device_id_type=MESH)
+        move.start()
+        move.wait()
+        out_ref[...] = fin[...]
+
+    @pl.when(turn % 2 == 0)
+    def _():
+        out_ref[...] = red[...]
 
     halo_up.wait_send()
     halo_dn.wait_send()
     for copy in (s_copy, w_copy):
-        for j in range(PARTS + PARTS // 2):
-            for way in (0, 1):
-                copy(way, j).wait_send()
-    for g in range(4):
+        for steps in (half, rest):
+            left_here(copy, steps)
+    for g in range(5):
         combine(g).wait_send()
 
     def drain(w, s, d, o):
-        @pl.when(o != 0)
+        @pl.when((o != 0) | (w == 3))
         def _():
             z_copy(w, s, d, z).wait_send()
 
-    for g in range(4):
+    for g in range(5):
         each(g, drain)
 
 
@@ -311,10 +351,10 @@
             dma((2,)), dma((2,)),
             dma((2, steps)), dma((2, steps)),
             dma((2, steps)), dma((2, steps)),
-            dma((4,)), dma((4,)),
+            dma((5,)), dma((5,)),
             dma((4, 4)), dma((16,)),
             dma((1,)), dma((1,)),
-            pltpu.SemaphoreType.REGULAR((3,)),
+            pltpu.SemaphoreType.REGULAR((4,)),
         ],
         compiler_params=pltpu.CompilerParams(
             collective_id=0, has_side_effects=True, vmem_limit_bytes=60 * 2**20),

time: 54.3 us -> 53.1 us (0.978)
  the two profiles are of different devices: /device:TPU:4 before, /device:TPU:12 now
where the time goes in v5:
time: 53.1 us; the launch traced here: 53 us
  Pallas kernels  51.6 us (97%)
  local copies, waits for them, and re-layouts  1.38 us (3%)
    pallas_call x1, Pallas kernels, on_device(): pl.pallas_call(kernel, out_shape=jax.ShapeDtypeStruct((64, width), jnp.fl...  51.6 us
    unnamed x1, local copies, waits for them, and re-layouts  1.38 us

profile of v5, /device:TPU:12, one launch (start us, length us, event | category | flops | bytes accessed | tf_op | source)
XLA Modules:
  0.0 53.0 jit_solution(6406872360146370769)
XLA Ops:
  0.0 51.6 %gram.1 = f32[64,128]{1,0:T(8,128)} custom-call(bf16[32,64,128]{2,1,0:T(8,128)(2,1)} %bitcast.2, s32[16,32]{1,0:T(8,128)} %bitcast.3, bf16[32,64,1024]{2,1,0:T(8,128)(2,1)} %mass_hbm.1), custom_call_target="tpu_custom_call" | custom-call | tf_op jit(solution)/shard_map/gram/pallas_call | solution.py:332
  51.6 1.4 %copy.5 = f32[64,128]{1,0:T(8,128)} copy(f32[64,128]{1,0:T(8,128)} %gram.1) | data formatting | bytes 65536

commit v6 on v5

--- a/solution.py
+++ b/solution.py
@@ -145,16 +145,16 @@
     have = set()
     for j in order:
         loads[j].wait()
-        lax.fori_loop(j * bpc, (j + 1) * bpc, weigh, 0, unroll=4)
+        lax.fori_loop(j * bpc, (j + 1) * bpc, weigh, 0, unroll=8)
         have.add(j)
         for way in (0, 1):
             while started[way] < PARTS // 2 and part_of(way, started[way]) in have:
                 w_copy(way, started[way]).start()
                 started[way] += 1
 
+    begin(w_copy, whole)
     begin(s_copy, whole)
     arrived(s_copy, half)
-    begin(w_copy, whole)
     pass_on(1)
     left_here(s_copy, whole)
     begin(s_copy, rest)

time: 53.1 us -> 52.6 us (level)
  no operation moved by 1% of the time
where the time goes in v6:
time: 52.6 us; the launch traced here: 52.4 us
  Pallas kernels  51.1 us (97%)
  local copies, waits for them, and re-layouts  1.38 us (3%)
    pallas_call x1, Pallas kernels, on_device(): pl.pallas_call(kernel, out_shape=jax.ShapeDtypeStruct((64, width), jnp.fl...  51.1 us
    unnamed x1, local copies, waits for them, and re-layouts  1.38 us

profile of v6, /device:TPU:12, one launch (start us, length us, event | category | flops | bytes accessed | tf_op | source)
XLA Modules:
  0.0 52.4 jit_solution(6661780034077089352)
XLA Ops:
  0.0 51.1 %gram.1 = f32[64,128]{1,0:T(8,128)} custom-call(bf16[32,64,128]{2,1,0:T(8,128)(2,1)} %bitcast.2, s32[16,32]{1,0:T(8,128)} %bitcast.3, bf16[32,64,1024]{2,1,0:T(8,128)(2,1)} %mass_hbm.1), custom_call_target="tpu_custom_call" | custom-call | tf_op jit(solution)/shard_map/gram/pallas_call | solution.py:332
  51.1 1.4 %copy.5 = f32[64,128]{1,0:T(8,128)} copy(f32[64,128]{1,0:T(8,128)} %gram.1) | data formatting | bytes 65536

commit v7 on v6

--- a/solution.py
+++ b/solution.py
@@ -188,7 +188,8 @@
         (3, lambda n: 1, lambda n: n, (1, three)),
         (3, lambda n: 2, lambda n: n, (2, three)),
         (3, lambda n: n, lambda n: 3, (three, 3)),
-        (4, lambda n: 3, lambda n: (z // 4 + along_x(n) + 7 - y) % 4, (3, pl.ds(0, 4))),
+        (2, lambda n: 3, lambda n: n, (3, pl.ds(0, 2))),
+        (2, lambda n: 3, lambda n: 2 + n, (3, pl.ds(2, 2))),
     )
 
     def combine(g):
@@ -225,7 +226,7 @@
             body(w, s, *chip(w, s))
             return 0
 
-        lax.fori_loop(0, groups[g][0], one, 0)
+        lax.fori_loop(0, groups[g][0], one, 0, unroll=True)
 
     def send(g):
         at = groups[g][3]
@@ -234,7 +235,7 @@
         put(coded, share[*at], *at)
 
         def one(w, s, d, o):
-            if g == 4:
+            if g >= 4:
                 z_copy(w, s, d, z, over).start()
             else:
                 @pl.when(o != 0)
@@ -266,12 +267,18 @@
     combine(3).start()
     pass_on(3)
     send(3)
-    for j in range(PARTS, PARTS + PARTS // 2):
+    for j in rest:
+        last = j == rest[-1]
         for way in (0, 1):
             w_copy(way, j, True).wait_recv()
-            gram_part(far, near + far, part_of(way, j), j == PARTS and way == 0)
-    combine(4).start()
+            if not last:
+                gram_part(far, near + far, part_of(way, j), j == PARTS and way == 0)
+    for g, ss in ((4, (0, 1)), (5, (2, 3))):
+        for way in (0, 1):
+            gram_part(far, ss, part_of(way, rest[-1]), False)
+        combine(g).start()
     send(4)
+    send(5)
 
     @pl.when(turn == 2)
     def _():
@@ -310,7 +317,7 @@
     for copy in (s_copy, w_copy):
         for steps in (half, rest):
             left_here(copy, steps)
-    for g in range(5):
+    for g in range(6):
         combine(g).wait_send()
 
     def drain(w, s, d, o):
@@ -318,7 +325,7 @@
         def _():
             z_copy(w, s, d, z).wait_send()
 
-    for g in range(5):
+    for g in range(6):
         each(g, drain)
 
 
@@ -351,7 +358,7 @@
             dma((2,)), dma((2,)),
             dma((2, steps)), dma((2, steps)),
             dma((2, steps)), dma((2, steps)),
-            dma((5,)), dma((5,)),
+            dma((6,)), dma((6,)),
             dma((4, 4)), dma((16,)),
             dma((1,)), dma((1,)),
             pltpu.SemaphoreType.REGULAR((4,)),

time: 52.6 us -> 52.2 us (level)
  no operation moved by 1% of the time
where the time goes in v7:
time: 52.2 us; the launch traced here: 52 us
  Pallas kernels  50.6 us (97%)
  local copies, waits for them, and re-layouts  1.38 us (3%)
    pallas_call x1, Pallas kernels, on_device(): pl.pallas_call(kernel, out_shape=jax.ShapeDtypeStruct((64, width), jnp.fl...  50.6 us
    unnamed x1, local copies, waits for them, and re-layouts  1.38 us

profile of v7, /device:TPU:12, one launch (start us, length us, event | category | flops | bytes accessed | tf_op | source)
XLA Modules:
  0.0 52.0 jit_solution(15995676683466360045)
XLA Ops:
  0.0 50.6 %gram.1 = f32[64,128]{1,0:T(8,128)} custom-call(bf16[32,64,128]{2,1,0:T(8,128)(2,1)} %bitcast.2, s32[16,32]{1,0:T(8,128)} %bitcast.3, bf16[32,64,1024]{2,1,0:T(8,128)(2,1)} %mass_hbm.1), custom_call_target="tpu_custom_call" | custom-call | tf_op jit(solution)/shard_map/gram/pallas_call | solution.py:339
  50.6 1.4 %copy.5 = f32[64,128]{1,0:T(8,128)} copy(f32[64,128]{1,0:T(8,128)} %gram.1) | data formatting | bytes 65536
